TPU v7x, 32 devices: a whole 2x2x4 slice. The times are simulated.
32 devices in a mesh: tm: 4 (over y, x), rows: 8 (over z, core).
Axes of the slice: x: 2, y: 2, z: 4, core: 2. Of those that a mesh axis runs over, the one named last changes fastest.
Arguments:
- latent: bfloat16 [4, 8, 160, 512], P('tm', 'rows'), may hold values from -350 to 350, as said below
- norm_gain: float32 [512], replicated, may hold values from 0.1 to 1.9
- norm_bias: float32 [512], replicated, may hold values from -4 to 4
- conv_weight: bfloat16 [3, 3, 3, 512, 512], P(None, None, None, 'rows', 'tm'), may hold values from -0.0546875 to 0.0546875
- cotangent: bfloat16 [4, 16, 320, 512], P('tm', 'rows'), may hold values from -180 to 180
Outputs:
- latent_grad: float32 [4, 8, 160, 512], P('tm', 'rows')
- gain_grad: float32 [512], replicated
- bias_grad: float32 [512], replicated
Inputs may be any that keep to these rules, and one draw needn't show every extreme that they name: `latent`: features of the unit's input.
All inputs are finite; a program needn't handle non-finite values.
Results may differ from a plain program's by a relative error of at most 0.0003.
Values may be sent and summed in bfloat16 or wider, within the bound.
A program may use at most 320 MiB of HBM per device.

v0:
```python
import jax
import jax.numpy as jnp
from jax import lax
from jax.sharding import PartitionSpec as P

GROUPS = 32


def extended(block, sides, width):
    for axis, dim in sides:
        count = lax.axis_size(axis)
        forward = [(i, i + 1) for i in range(count - 1)]
        backward = [(target, source) for source, target in forward]
        low = lax.ppermute(
            lax.slice_in_dim(block, block.shape[dim] - width, None, axis=dim), axis, forward
        )
        high = lax.ppermute(lax.slice_in_dim(block, 0, width, axis=dim), axis, backward)
        block = jnp.concatenate([low, block, high], axis=dim)
    return block


def from_behind(value, axis, steps):
    count = lax.axis_size(axis)
    first, last = (max(0, -steps), min(count, count - steps))
    return lax.ppermute(value, axis, [(source, source + steps) for source in range(first, last)])


def shifted_rows(frames, extra_frames):
    padded = jnp.pad(frames, ((0, extra_frames), (0, 0), (1, 1), (0, 0)))
    fine_rows = frames.shape[1] - 2
    return [padded[:, 2 - row_tap : 2 - row_tap + fine_rows] for row_tap in range(3)]


def tap_total(row_slabs, weights, tap_pairs, frames_out, span_cols):
    running = None
    for offset, tap_index in tap_pairs:
        for row_tap in range(3):
            source = row_slabs[row_tap][offset : offset + frames_out]
            for col_tap in range(3):
                product = lax.dot_general(
                    source,
                    weights[tap_index, row_tap, col_tap],
                    (((3,), (1,)), ((), ())),
                    preferred_element_type=jnp.float32,
                )
                piece = product[:, :, 2 - col_tap : 2 - col_tap + span_cols, :]
                running = piece if running is None else running + piece
    return running


def pool_pairs(fine_grad):
    frames, fine_rows, span_cols, channels = fine_grad.shape
    return fine_grad.reshape(frames, fine_rows // 2, 2, span_cols // 2, 2, channels).sum(
        axis=(2, 4)
    )


def block_grad(row_slabs, weights, frames_out, first_frame):
    span_cols = row_slabs[0].shape[2] - 2

    def extra_terms():
        return tap_total(row_slabs, weights, ((0, 1), (0, 0), (1, 0)), 1, span_cols)

    def no_terms():
        return jnp.zeros((1, row_slabs[0].shape[1], span_cols, weights.shape[3]), jnp.float32)

    main_part = tap_total(row_slabs, weights, ((0, 2), (1, 1), (2, 0)), frames_out, span_cols)
    main_part = main_part + lax.cond(first_frame, extra_terms, no_terms)
    return pool_pairs(main_part)


def on_device(latent, norm_gain, norm_bias, conv_weight, cotangent):
    frames_all = lax.axis_size("tm")
    rows_all = lax.axis_size("rows")
    low_rows = latent.shape[1]
    low_cols = latent.shape[2]
    channels = latent.shape[3]
    per_group = channels // GROUPS
    cell_count = frames_all * rows_all * low_rows * low_cols
    rimmed = extended(cotangent, (("rows", 1),), 1)
    following = from_behind(rimmed, "tm", -1)
    further = from_behind(rimmed, "tm", -2)
    stacked = jnp.concatenate([rimmed, following, further], axis=0)
    weight_wide = lax.all_gather(conv_weight, "tm", axis=4, tiled=True)
    weight_full = lax.all_gather(weight_wide, "rows", axis=3, tiled=True)
    up_grad = block_grad(shifted_rows(stacked, 0), weight_full, 1, lax.axis_index("tm") == 0)
    features = latent.astype(jnp.float32)
    sum_x = jnp.sum(features, axis=(0, 1, 2))
    sum_sq = jnp.sum(features * features, axis=(0, 1, 2))
    total_x, total_sq = lax.psum((sum_x, sum_sq), ("tm", "rows"))
    group_x = total_x.reshape(GROUPS, per_group).sum(axis=1)
    group_sq = total_sq.reshape(GROUPS, per_group).sum(axis=1)
    group_mean = group_x / (cell_count * per_group)
    group_var = group_sq / (cell_count * per_group) - group_mean * group_mean
    inv_std = lax.rsqrt(group_var + 1e-06)
    mean_chan = jnp.repeat(group_mean, per_group)
    inv_chan = jnp.repeat(inv_std, per_group)
    normed = (features - mean_chan) * inv_chan
    pre = normed * norm_gain + norm_bias
    sigmoid_pre = jax.nn.sigmoid(pre)
    act_grad = up_grad * sigmoid_pre * (1.0 + pre * (1.0 - sigmoid_pre))
    sum_act, sum_scaled = lax.psum(
        (jnp.sum(act_grad, axis=(0, 1, 2)), jnp.sum(act_grad * normed, axis=(0, 1, 2))),
        ("tm", "rows"),
    )
    gain_grad = sum_scaled / cell_count
    bias_grad = sum_act / cell_count
    mean_q = (norm_gain * sum_act).reshape(GROUPS, per_group).sum(axis=1) / (cell_count * per_group)
    mean_qn = (norm_gain * sum_scaled).reshape(GROUPS, per_group).sum(axis=1) / (
        cell_count * per_group
    )
    latent_grad = inv_chan * (
        act_grad * norm_gain
        - jnp.repeat(mean_q, per_group)
        - normed * jnp.repeat(mean_qn, per_group)
    )
    return (latent_grad, gain_grad, bias_grad)


def solution(mesh):
    placed = (
        P("tm", "rows", None, None),
        P(),
        P(),
        P(None, None, None, "rows", "tm"),
        P("tm", "rows", None, None),
    )
    return jax.shard_map(
        on_device,
        mesh=mesh,
        in_specs=placed,
        out_specs=(P("tm", "rows", None, None), P(), P()),
        check_vma=False,
    )
```

profile of v0, /device:TPU:0, one launch (start us, length us, event | category | flops | bytes accessed | tf_op | source)
XLA Modules:
  0.0 324.7 jit_solution(18014490503378424369)
XLA Ops:
  8.0 37.1 %all-gather.3.cloned.1.call-done = bf16[3,3,3,64,512]{4,3,2,1,0:T(8,128)(2,1)} async-done(((bf16[3,3,3,64,128]{4,3,2,1,0:T(8,128)(2,1)}), bf16[3,3,3,64,512]{4,3,2,1,0:T(8,128)(2,1)}) %all-gather.3.cloned.1.call-update) | async-done | bytes 1769488 | tf_op jit(solution)/shard_map/all_gather | solution.py:84
  45.1 1.9 collective-permute-start
  48.4 3.4 %collective-permute-done.1 = bf16[1,1,320,512]{3,2,1,0:T(8,128)(2,1)S(1)} collective-permute-done((bf16[1,1,320,512]{3,2,1,0:T(8,128)(2,1)S(1)}, bf16[1,1,320,512]{3,2,1,0:T(8,128)(2,1)S(1)}, u32[]{:S(2)}, u32[]{:S(2)}) %collective-permute-start.1) | collective-permute-done | bytes 327712 | tf_op jit(solution)/shard_map/ppermute | solution.py:17
  54.7 102.3 %all-reduce.2 = (f32[32,16]{1,0:T(8,128)S(1)}, f32[32,16]{1,0:T(8,128)S(1)}) all-reduce(f32[32,16]{1,0:T(8,128)S(1)} %reshape.178, f32[32,16]{1,0:T(8,128)S(1)} %reshape.177), channel_id=1, replica_groups=mesh['tm'=4,'rows'=8] {'tm','rows'}, use_global_device_ids=true, to_apply=%region_4.5 | all-reduce | flops 1024 | bytes 8192 | tf_op jit(solution)/shard_map/psum | solution.py:90
  157.5 3.9 %fusion.113 = bf16[3,4,322,512]{3,2,1,0:T(8,128)(2,1)} fusion(bf16[1,4,320,512]{3,2,1,0:T(8,128)(2,1)} %collective-permute-done.3, bf16[1,4,320,512]{3,2,1,0:T(8,128)(2,1)} %collective-permute-done.2, bf16[1,4,320,512]{3,2,1,0:T(8,128)(2,1)S(1)} %constant_dynamic-update-slice_fusion), kind=kLoop, calls=%fused_computation.168 | loop fusion | flops 23740416 | bytes 7888896 | tf_op jit(solution)/shard_map/concatenate | solution.py:83
  161.4 15.9 %all-gather.5.cloned.1.call-done = bf16[3,3,3,512,512]{4,3,2,1,0:T(8,128)(2,1)} async-done(((bf16[3,3,3,64,512]{4,3,2,1,0:T(8,128)(2,1)}), bf16[3,3,3,512,512]{4,3,2,1,0:T(8,128)(2,1)}) %all-gather.5.cloned.1.call-update) | async-done | bytes 14155792 | tf_op jit(solution)/shard_map/all_gather | solution.py:85
  177.3 48.1 %conditional.1 = (f32[1,2,320,512]{3,2,1,0:T(8,128)}) conditional(s32[]{:T(128)} %convert_element_type.9, () %tuple.14, (bf16[3,4,322,512]{3,2,1,0:T(8,128)(2,1)}, bf16[3,3,3,512,512]{4,3,2,1,0:T(8,128)(2,1)}) %tuple.15), branch_computations={%region_6.7_spmd, %region_7.8_spmd} | conditional | flops 9124839424 | bytes 177053760 | solution.py:68
  177.3 1.9 convolution_bitcast_fusion.15
  179.3 1.8 convolution_bitcast_fusion.16
  181.1 1.7 convolution_bitcast_fusion.17
  182.8 2.0 convolution_bitcast_fusion.24
  184.9 2.1 convolution_bitcast_fusion.25
  208.1 1.7 convolution_bitcast_fusion.5
  209.8 1.7 convolution_bitcast_fusion.8
  216.4 9.0 %slice_add_fusion = f32[1,2,320,512]{3,2,1,0:T(8,128)} fusion(f32[1,2,322,512]{3,2,1,0:T(8,128)} %convolution_bitcast_fusion, f32[1,2,322,512]{3,2,1,0:T(8,128)} %convolution_bitcast_fusion.1, f32[1,2,322,512]{3,2,1,0:T(8,128)} %convolution_bitcast_fusion.2, f32[1,2,322,512]{3,2,1,0:T(8,128)} %convolution_bitcast_fusion.3, ...), kind=kLoop, calls=%fused_computation.27 | loop fusion | flops 8519680 | bytes 36700160 | tf_op jit(solution)/shard_map/cond/branch_1_fun/add | solution.py:47
  225.4 1.9 convolution_bitcast_fusion.28
  227.4 1.8 convolution_bitcast_fusion.27
  229.2 1.7 convolution_bitcast_fusion.31
  230.9 2.0 convolution_bitcast_fusion.30
  233.0 2.1 convolution_bitcast_fusion.34
  242.6 1.7 convolution_bitcast_fusion.45
  244.3 1.7 convolution_bitcast_fusion.49
  265.5 10.1 %fusion.115 = f32[320,512]{1,0:T(8,128)} fusion(f32[1,2,320,512]{3,2,1,0:T(8,128)} %get-tuple-element.34, f32[1,2,322,512]{3,2,1,0:T(8,128)S(1)} %convolution_bitcast_fusion.27, f32[1,2,322,512]{3,2,1,0:T(8,128)S(1)} %convolution_bitcast_fusion.28, f32[1,2,322,512]{3,2,1,0:T(8,128)} %convolution_bitcast_fusion.29, ...), kind=kLoop, calls=%fused_computation.198 | loop fusion | flops 9011200 | bytes 37355520 | tf_op jit(solution)/shard_map/reduce_sum | solution.py:53
  278.2 37.6 %all-reduce.1 = (f32[512]{0:T(512)S(1)}, f32[512]{0:T(512)S(1)}) all-reduce(f32[512]{0:T(512)S(1)} %get-tuple-element.18, f32[512]{0:T(512)S(1)} %get-tuple-element.17), channel_id=1, replica_groups=mesh['tm'=4,'rows'=8] {'tm','rows'}, use_global_device_ids=true, to_apply=%region_14.15 | all-reduce | flops 1024 | bytes 8192 | tf_op jit(solution)/shard_map/psum | solution.py:102
  (95 shorter events, 63.0 us)
Async XLA Ops:
  7.2 37.9 %copy-start.4 = (bf16[1,2,320,512]{3,2,1,0:T(8,128)(2,1)S(1)}, bf16[1,2,320,512]{3,2,1,0:T(8,128)(2,1)}, u32[]{:S(2)}) copy-start(bf16[1,2,320,512]{3,2,1,0:T(8,128)(2,1)} %param.11) | copy-start | bytes 1966084
  7.2 37.8 %all-gather.3.cloned.1.call-start = ((), (), s32[]{:S(2)}) async-start(), calls=%async_computation | async-start | bytes 2211840 | tf_op jit(solution)/shard_map/all_gather | solution.py:84
  7.9 169.4 %all-gather.5.cloned.1.call-start = ((), (), s32[]{:S(2)}) async-start(), calls=%async_computation.1 | async-start | bytes 15925248 | tf_op jit(solution)/shard_map/all_gather | solution.py:85
  45.1 9.3 %copy-start.5 = (bf16[1,1,160,512]{3,2,1,0:T(8,128)(2,1)S(1)}, bf16[1,1,160,512]{3,2,1,0:T(8,128)(2,1)}, u32[]{:S(2)}) copy-start(bf16[1,1,160,512]{3,2,1,0:T(8,128)(2,1)} %param.7) | copy-start | bytes 491524
  45.1 3.2 collective-permute-start
  47.0 4.8 %collective-permute-start.1 = (bf16[1,1,320,512]{3,2,1,0:T(8,128)(2,1)S(1)}, bf16[1,1,320,512]{3,2,1,0:T(8,128)(2,1)S(1)}, u32[]{:S(2)}, u32[]{:S(2)}) collective-permute-start(bf16[1,1,320,512]{3,2,1,0:T(8,128)(2,1)S(1)} %get-tuple-element.26), channel_id=1, source_target_pairs={{1,0},{2,1},{3,2},{4,3},{5,4},{6,5},{7,6},{9,8},{10,9},{11,10},{12... | collective-permute-start | bytes 983048 | tf_op jit(solution)/shard_map/ppermute | solution.py:17
  51.8 105.7 %collective-permute-start.3 = (bf16[1,4,320,512]{3,2,1,0:T(8,128)(2,1)S(1)}, bf16[1,4,320,512]{3,2,1,0:T(8,128)(2,1)}, u32[]{:S(2)}, u32[]{:S(2)}) collective-permute-start(bf16[1,4,320,512]{3,2,1,0:T(8,128)(2,1)S(1)} %constant_dynamic-update-slice_fusion), channel_id=1, source_target_pairs={{16,0},{24,8},{17,1},{25,9},{18,2},{26,10},{19,3},{27,11},{20,4},{... | collective-permute-start | bytes 3932168 | tf_op jit(solution)/shard_map/ppermute | solution.py:25
  53.1 104.4 %collective-permute-start.2 = (bf16[1,4,320,512]{3,2,1,0:T(8,128)(2,1)S(1)}, bf16[1,4,320,512]{3,2,1,0:T(8,128)(2,1)}, u32[]{:S(2)}, u32[]{:S(2)}) collective-permute-start(bf16[1,4,320,512]{3,2,1,0:T(8,128)(2,1)S(1)} %constant_dynamic-update-slice_fusion), channel_id=1, source_target_pairs={{8,0},{16,8},{24,16},{9,1},{17,9},{25,17},{10,2},{18,10},{26,18},{... | collective-permute-start | bytes 3932168 | tf_op jit(solution)/shard_map/ppermute | solution.py:25
  177.3 3.7 %copy-start.1 = (bf16[3,4,322,512]{3,2,1,0:T(8,128)(2,1)S(1)}, bf16[3,4,322,512]{3,2,1,0:T(8,128)(2,1)}, u32[]{:S(2)}) copy-start(bf16[3,4,322,512]{3,2,1,0:T(8,128)(2,1)} %get-tuple-element.12) | copy-start | bytes 11870212 | tf_op jit(solution)/shard_map/cond
  181.1 10.7 %copy-start.3 = (bf16[3,3,3,512,512]{4,3,2,1,0:T(8,128)(2,1)S(1)}, bf16[3,3,3,512,512]{4,3,2,1,0:T(8,128)(2,1)}, u32[]{:S(2)}) copy-start(bf16[3,3,3,512,512]{4,3,2,1,0:T(8,128)(2,1)} %get-tuple-element.13) | copy-start | bytes 42467332 | tf_op jit(solution)/shard_map/cond
  225.4 3.7 %copy-start = (bf16[3,4,322,512]{3,2,1,0:T(8,128)(2,1)S(1)}, bf16[3,4,322,512]{3,2,1,0:T(8,128)(2,1)}, u32[]{:S(2)}) copy-start(bf16[3,4,322,512]{3,2,1,0:T(8,128)(2,1)} %fusion.113) | copy-start | bytes 11870212
  229.2 10.7 %copy-start.2 = (bf16[3,3,3,512,512]{4,3,2,1,0:T(8,128)(2,1)S(1)}, bf16[3,3,3,512,512]{4,3,2,1,0:T(8,128)(2,1)}, u32[]{:S(2)}) copy-start(bf16[3,3,3,512,512]{4,3,2,1,0:T(8,128)(2,1)} %all-gather.5.cloned.1.call-done) | copy-start | bytes 42467332
  275.7 2.3 copy-start.6
  275.7 2.3 copy-start.7
Sparse Core Ops, SparseCore 0:
  9.8 35.1 all-gather.2
  46.6 130.6 all-gather.4
where the time goes:
time: 325 us
  blocking collectives  140 us (43%)
  matrix products  78.8 us (24%)
  waiting for transfers between devices  57.1 us (18%)
  other arithmetic  26 us (8%)
  between operations  14.4 us (4%)
  starting transfers between devices  5.84 us (2%)
    psum x1, blocking collectives, on_device(): total_x, total_sq = lax.psum((sum_x, sum_sq), ('tm', 'rows'))  102 us
    dot_general x54, matrix products, tap_total(): lax.dot_general(source, weights[tap_index, row_tap, col_tap], (((3,), (1,...  78.8 us
    psum x1, blocking collectives, on_device(): lax.psum((jnp.sum(act_grad, axis=(0, 1, 2)), jnp.sum(act_grad * normed, a...  37.6 us
    all_gather x1, waiting for transfers between devices, on_device(): weight_wide = lax.all_gather(conv_weight, 'tm', axis=4, tiled=True)  37.1 us
    all_gather x1, waiting for transfers between devices, on_device(): weight_full = lax.all_gather(weight_wide, 'rows', axis=3, tiled=True)  15.9 us
    reduce_sum x2, other arithmetic, pool_pairs(): fine_grad.reshape(frames, fine_rows // 2, 2, span_cols // 2, 2, channels)  10.9 us
    add x1, other arithmetic, tap_total(): running = piece if running is None else running + piece  9.05 us
  transfers between devices with their start and end apart: 6, of which 3 were waited for; matrix products, arithmetic and copies ran while one was open for 1% of the time, Pallas kernels for 0%

commit v1 on v0

v1 whole, which is shorter than its diff:
```python
import jax
import jax.numpy as jnp
from jax import lax
from jax.sharding import PartitionSpec as P

GROUPS = 32


def split_pair(value):
    high = lax.reduce_precision(value, 8, 7)
    return high.astype(jnp.bfloat16), (value - high).astype(jnp.bfloat16)


def row_rims(block):
    count = lax.axis_size("rows")
    forward = [(i, i + 1) for i in range(count - 1)]
    backward = [(target, source) for source, target in forward]
    low = lax.ppermute(block[:, -1:], "rows", forward)
    high = lax.ppermute(block[:, :1], "rows", backward)
    return jnp.concatenate([low, block, high], axis=1)


def box_sums(block):
    wide = jnp.pad(block.astype(jnp.float32), ((0, 0), (0, 0), (1, 1), (0, 0)))
    rows = wide[:, :-1] + wide[:, 1:]
    return rows[:, :, :-1] + rows[:, :, 1:]


def up_grad_part(boxes, weights, low_rows, low_cols):
    frames = boxes.shape[0]
    early = [boxes[:1]]
    for t in (1, 2):
        early.append(early[-1] + boxes[t : t + 1])
    total = None
    for a in range(3):
        stack = jnp.concatenate([early[2 - a], boxes[3 - a :]], axis=0)
        taps = []
        for b in range(3):
            for c in range(3):
                taps.append(
                    stack[:, 2 - b : 1 - b + 2 * low_rows : 2, 2 - c : 1 - c + 2 * low_cols : 2]
                )
        wide = jnp.concatenate(taps, axis=-1)
        kernel = jnp.concatenate([weights[a, b, c] for b in range(3) for c in range(3)], axis=-1)
        high, low = split_pair(wide)
        product = sum(
            lax.dot_general(
                part, kernel, (((3,), (1,)), ((), ())), preferred_element_type=jnp.float32
            )
            for part in (high, low)
        )
        product = jnp.pad(product, ((0, frames - product.shape[0]), (0, 0), (0, 0), (0, 0)))
        total = product if total is None else total + product
    return total


def spread_out(latent, norm_gain, norm_bias, conv_weight, cotangent):
    frames_all = lax.axis_size("tm")
    rows_all = lax.axis_size("rows")
    low_rows, low_cols, channels = latent.shape[1:]
    per_group = channels // GROUPS
    cell_count = frames_all * rows_all * low_rows * low_cols
    weights = lax.all_gather(conv_weight, "rows", axis=3, tiled=True)
    swapped = lax.all_to_all(cotangent, "tm", split_axis=3, concat_axis=0, tiled=True)
    part = up_grad_part(box_sums(row_rims(swapped)), weights, low_rows, low_cols)
    up_grad = lax.psum_scatter(part, "tm", scatter_dimension=0, tiled=True)
    features = latent.astype(jnp.float32)
    sum_x = jnp.sum(features, axis=(0, 1, 2))
    sum_sq = jnp.sum(features * features, axis=(0, 1, 2))
    total_x, total_sq = lax.psum((sum_x, sum_sq), ("tm", "rows"))
    group_x = total_x.reshape(GROUPS, per_group).sum(axis=1)
    group_sq = total_sq.reshape(GROUPS, per_group).sum(axis=1)
    group_mean = group_x / (cell_count * per_group)
    group_var = group_sq / (cell_count * per_group) - group_mean * group_mean
    inv_std = lax.rsqrt(group_var + 1e-06)
    mean_chan = jnp.repeat(group_mean, per_group)
    inv_chan = jnp.repeat(inv_std, per_group)
    normed = (features - mean_chan) * inv_chan
    pre = normed * norm_gain + norm_bias
    sigmoid_pre = jax.nn.sigmoid(pre)
    act_grad = up_grad * sigmoid_pre * (1.0 + pre * (1.0 - sigmoid_pre))
    sum_act, sum_scaled = lax.psum(
        (jnp.sum(act_grad, axis=(0, 1, 2)), jnp.sum(act_grad * normed, axis=(0, 1, 2))),
        ("tm", "rows"),
    )
    gain_grad = sum_scaled / cell_count
    bias_grad = sum_act / cell_count
    mean_q = (norm_gain * sum_act).reshape(GROUPS, per_group).sum(axis=1) / (cell_count * per_group)
    mean_qn = (norm_gain * sum_scaled).reshape(GROUPS, per_group).sum(axis=1) / (
        cell_count * per_group
    )
    latent_grad = inv_chan * (
        act_grad * norm_gain
        - jnp.repeat(mean_q, per_group)
        - normed * jnp.repeat(mean_qn, per_group)
    )
    return (latent_grad, gain_grad, bias_grad)


def solution(mesh):
    placed = (
        P("tm", "rows", None, None),
        P(),
        P(),
        P(None, None, None, "rows", "tm"),
        P("tm", "rows", None, None),
    )
    return jax.shard_map(
        spread_out,
        mesh=mesh,
        in_specs=placed,
        out_specs=(P("tm", "rows", None, None), P(), P()),
        check_vma=False,
    )
```

time: 325 us -> 194 us (0.60)
  matrix products: 78.8 us -> 12.6 us
  waiting for transfers between devices: 57.1 us -> 3.97 us
  local copies, waits for them, and re-layouts: 2.58 us -> 53.4 us
  blocking collectives: 140 us -> 100 us
  other arithmetic: 26 us -> 6.04 us
    dot_general x54 -> x6, matrix products: 78.8 us -> 12.6 us  [up_grad_part(): lax.dot_general(part, kernel, (((3,), (1,)), ((), ())), preferred_element...]
    psum x2, blocking collectives: 140 us -> 83.9 us  [the longest x1 44.3 us: spread_out(): total_x, total_sq = lax.psum((sum_x, sum_sq), ('tm', 'rows'))]
    all_gather x2 -> x1, waiting for transfers between devices: 53 us -> 0.01 us  [spread_out(): weights = lax.all_gather(conv_weight, 'rows', axis=3, tiled=True)]
    unnamed x14 -> x77, local copies, waits for them, and re-layouts: 0.09 us -> 30 us
    slice x1 -> x30, local copies, waits for them, and re-layouts: 0.04 us -> 18.6 us  [the longest x27 18.1 us: up_grad_part(): stack[:, 2 - b:1 - b + 2 * low_rows:2, 2 - c:1 - c + 2 * low_cols:2]]
    all_to_all x0 -> x1, blocking collectives: none -> 16.3 us  [spread_out(): lax.all_to_all(cotangent, 'tm', split_axis=3, concat_axis=0, tiled=True)]
    reduce_sum x8 -> x6, other arithmetic: 11.6 us -> 1.71 us  [the longest x1 1.18 us: spread_out(): jnp.sum(act_grad, axis=(0, 1, 2))]
    add x1 -> x3, other arithmetic: 9.05 us -> 1.4 us  [the longest x1 1.05 us: up_grad_part(): early.append(early[-1] + boxes[t:t + 1])]
  transfers between devices with their start and end apart: 6 -> 4, of which waited for: 3 -> 1; matrix products, arithmetic and copies ran while one was open for 1% -> 21% of each run, Pallas kernels for 0% -> 0%
where the time goes in v1:
time: 194 us; the launch traced here: 193 us
  blocking collectives  100 us (52%)
  local copies, waits for them, and re-layouts  53.4 us (28%)
  between operations  14.5 us (7%)
  matrix products  12.6 us (6%)
  other arithmetic  6.04 us (3%)
  waiting for transfers between devices  3.97 us (2%)
  starting transfers between devices  2.68 us (1%)
    psum x1, blocking collectives, spread_out(): total_x, total_sq = lax.psum((sum_x, sum_sq), ('tm', 'rows'))  44.3 us
    psum x1, blocking collectives, spread_out(): lax.psum((jnp.sum(act_grad, axis=(0, 1, 2)), jnp.sum(act_grad * normed, a...  39.6 us
    unnamed x77, local copies, waits for them, and re-layouts  30 us
    slice x27, local copies, waits for them, and re-layouts, up_grad_part(): stack[:, 2 - b:1 - b + 2 * low_rows:2, 2 - c:1 - c + 2 * low_cols:2]  18.1 us
    all_to_all x1, blocking collectives, spread_out(): lax.all_to_all(cotangent, 'tm', split_axis=3, concat_axis=0, tiled=True)  16.3 us
    dot_general x6, matrix products, up_grad_part(): lax.dot_general(part, kernel, (((3,), (1,)), ((), ())), preferred_element...  12.6 us
    ppermute x1, waiting for transfers between devices, row_rims(): high = lax.ppermute(block[:, :1], 'rows', backward)  3.93 us
  transfers between devices with their start and end apart: 4, of which 1 were waited for; matrix products, arithmetic and copies ran while one was open for 21% of the time, Pallas kernels for 0%

profile of v1, /device:TPU:0, one launch (start us, length us, event | category | flops | bytes accessed | tf_op | source)
XLA Modules:
  0.0 193.3 jit_solution(6387797435812883643)
XLA Ops:
  7.2 2.6 %copy.14 = bf16[1,2,320,512]{2,1,0,3:T(2,128)(2,1)S(1)} copy(bf16[1,2,320,512]{3,2,1,0:T(8,128)(2,1)} %param.9) | data formatting | bytes 1310720 | tf_op args[4]
  9.8 16.3 %all_to_all.18 = bf16[1,2,320,512]{2,1,0,3:T(2,128)(2,1)S(1)} all-to-all(bf16[1,2,320,512]{2,1,0,3:T(2,128)(2,1)S(1)} %copy.14), channel_id=1, replica_groups=mesh['tm'=4,'rows'=8] {'tm'}, dimensions={3} | all-to-all | bytes 1310720 | tf_op jit(solution)/shard_map/all_to_all | solution.py:64
  26.1 1.2 copy.16
  27.4 1.3 collective-permute-start
  28.7 1.3 collective-permute-start.1
  30.1 3.9 %collective-permute-done.1 = bf16[4,1,320,128]{3,2,0,1:T(8,128)(2,1)S(1)} collective-permute-done((bf16[4,1,320,128]{3,2,0,1:T(8,128)(2,1)S(1)}, bf16[4,1,320,128]{3,2,0,1:T(8,128)(2,1)S(1)}, u32[]{:S(2)}, u32[]{:S(2)}) %collective-permute-start.1) | collective-permute-done | bytes 327712 | tf_op jit(solution)/shard_map/ppermute | solution.py:19
  37.4 1.1 pad_maximum_fusion
  56.7 1.7 bitcast_dynamic-update-slice_fusion.25
  58.4 1.6 bitcast_dynamic-update-slice_fusion.24
  60.0 1.7 bitcast_dynamic-update-slice_fusion.23
  61.7 1.7 bitcast_dynamic-update-slice_fusion.22
  63.4 1.6 bitcast_dynamic-update-slice_fusion.21
  76.8 1.1 fusion.70
  77.9 1.1 fusion.69
  79.1 1.1 fusion.68
  80.2 1.1 fusion.67
  82.4 1.1 fusion.65
  85.8 2.0 %fusion.24 = f32[2,160,512]{2,1,0:T(8,128)S(1)} fusion(bf16[512,1152]{1,0:T(8,128)(2,1)S(1)} %get-tuple-element.23, f32[2,160,1152]{2,1,0:T(8,128)} %bitcast_dynamic-update-slice_fusion.18), kind=kOutput, calls=%fused_computation.36 | convolution fusion | flops 378224640 | bytes 3309568 | tf_op jit(solution)/shard_map/dot_general | solution.py:47
  87.8 2.0 %fusion.17 = f32[2,1,160,512]{3,2,0,1:T(8,128)S(1)} fusion(f32[2,160,512]{2,1,0:T(8,128)S(1)} %fusion.24, bf16[512,1152]{1,0:T(8,128)(2,1)S(1)} %get-tuple-element.23, f32[2,160,1152]{2,1,0:T(8,128)} %bitcast_dynamic-update-slice_fusion.18), kind=kOutput, calls=%fused_computation.29 | convolution fusion | flops 378757120 | bytes 3964928 | tf_op jit(solution)/shard_map/dot_general | solution.py:47
  91.6 2.9 %fusion.7 = f32[4,160,512]{2,1,0:T(8,128)S(1)} fusion(f32[4,160,1152]{2,1,0:T(8,128)} %bitcast_dynamic-update-slice_fusion, bf16[512,1152]{1,0:T(8,128)(2,1)S(1)} %get-tuple-element.24), kind=kOutput, calls=%fused_computation.18 | convolution fusion | flops 757186560 | bytes 5439488 | tf_op jit(solution)/shard_map/dot_general | solution.py:47
  94.5 4.0 %fusion.12 = f32[4,1,160,512]{3,2,0,1:T(8,128)} fusion(f32[4,160,512]{2,1,0:T(8,128)S(1)} %fusion.7, f32[4,160,1152]{2,1,0:T(8,128)} %bitcast_dynamic-update-slice_fusion, f32[3,1,160,512]{3,2,0,1:T(8,128)S(1)} %fusion.13, f32[2,1,160,512]{3,2,0,1:T(8,128)S(1)} %fusion.17, bf16[512,1152]{1,0:T(8,128)(2,1)S(1)} %get-tuple-element.24), kind=kOutput, calls=%fused_computation.22 | convolution fusion | flops 757432320 | bytes 8388608 | tf_op jit(solution)/shard_map/dot_general | solution.py:47
  98.7 44.3 %all-reduce.5 = (f32[32,16]{1,0:T(8,128)S(1)}, f32[32,16]{1,0:T(8,128)S(1)}) all-reduce(f32[32,16]{1,0:T(8,128)S(1)} %reshape.442, f32[32,16]{1,0:T(8,128)S(1)} %reshape.441), channel_id=1, replica_groups=mesh['tm'=4,'rows'=8] {'tm','rows'}, use_global_device_ids=true, to_apply=%region_4.5 | all-reduce | flops 1024 | bytes 8192 | tf_op jit(solution)/shard_map/psum | solution.py:70
  143.6 1.2 fusion.72
  144.8 39.6 %all-reduce.4 = (f32[512]{0:T(512)S(1)}, f32[512]{0:T(512)S(1)}) all-reduce(f32[512]{0:T(512)S(1)} %get-tuple-element.13, f32[512]{0:T(512)S(1)} %get-tuple-element.12), channel_id=1, replica_groups=mesh['tm'=4,'rows'=8] {'tm','rows'}, use_global_device_ids=true, to_apply=%region_11.12 | all-reduce | flops 1024 | bytes 8192 | tf_op jit(solution)/shard_map/psum | solution.py:82
  (136 shorter events, 41.2 us)
Async XLA Ops:
  7.2 68.5 %all-gather.2.cloned.1.call-start = ((), (), s32[]{:S(2)}) async-start(), calls=%async_computation.2 | async-start | bytes 3981312 | tf_op jit(solution)/shard_map/all_gather | solution.py:63
  27.4 2.7 %collective-permute-start = (bf16[4,1,320,128]{3,2,0,1:T(8,128)(2,1)S(1)}, bf16[4,1,320,128]{3,2,0,1:T(8,128)(2,1)S(1)}, u32[]{:S(2)}, u32[]{:S(2)}) collective-permute-start(bf16[4,1,320,128]{3,2,0,1:T(8,128)(2,1)S(1)} %get-tuple-element.51), channel_id=1, source_target_pairs={{0,1},{1,2},{2,3},{3,4},{4,5},{5,6},{6,7},{8,9},{9,10},{10,11},{11... | collective-permute-start | bytes 983048 | tf_op jit(solution)/shard_map/ppermute | solution.py:18
  28.7 5.3 %collective-permute-start.1 = (bf16[4,1,320,128]{3,2,0,1:T(8,128)(2,1)S(1)}, bf16[4,1,320,128]{3,2,0,1:T(8,128)(2,1)S(1)}, u32[]{:S(2)}, u32[]{:S(2)}) collective-permute-start(bf16[4,1,320,128]{3,2,0,1:T(8,128)(2,1)S(1)} %get-tuple-element.52), channel_id=1, source_target_pairs={{1,0},{2,1},{3,2},{4,3},{5,4},{6,5},{7,6},{9,8},{10,9},{11,10},{12... | collective-permute-start | bytes 983048 | tf_op jit(solution)/shard_map/ppermute | solution.py:19
  30.0 113.5 %reduce-scatter.7.cloned.1.call-start = ((), (), s32[]{:S(2)}) async-start(), calls=%async_computation.3 | async-start | bytes 1638400
  34.7 1.4 copy-start
  36.1 1.3 slice-start
  46.8 5.3 %copy-start.1 = (f32[4,3,321,128]{3,2,0,1:T(8,128)S(1)}, f32[4,3,321,128]{3,2,0,1:T(8,128)}, u32[]{:S(2)}) copy-start(f32[4,3,321,128]{3,2,0,1:T(8,128)} %copy-done) | copy-start | bytes 5916676
  56.5 9.9 %copy-start.17 = (f32[2,1,160,128]{3,2,0,1:T(8,128)S(1)}, f32[2,1,160,128]{3,2,0,1:T(8,128)}, u32[]{:S(2)}) copy-start(f32[2,1,160,128]{3,2,0,1:T(8,128)} %slice.242) | copy-start | bytes 491524
  56.7 8.3 %copy-start.19 = (f32[2,1,160,128]{3,2,0,1:T(8,128)S(1)}, f32[2,1,160,128]{3,2,0,1:T(8,128)}, u32[]{:S(2)}) copy-start(f32[2,1,160,128]{3,2,0,1:T(8,128)} %slice.240) | copy-start | bytes 491524
  56.7 9.0 %copy-start.18 = (f32[2,1,160,128]{3,2,0,1:T(8,128)S(1)}, f32[2,1,160,128]{3,2,0,1:T(8,128)}, u32[]{:S(2)}) copy-start(f32[2,1,160,128]{3,2,0,1:T(8,128)} %slice.241) | copy-start | bytes 491524
  56.7 10.5 %copy-start.16 = (f32[3,1,160,128]{3,2,0,1:T(8,128)S(1)}, f32[3,1,160,128]{3,2,0,1:T(8,128)}, u32[]{:S(2)}) copy-start(f32[3,1,160,128]{3,2,0,1:T(8,128)} %slice.253) | copy-start | bytes 737284
  56.7 10.5 %copy-start.15 = (f32[3,1,160,128]{3,2,0,1:T(8,128)S(1)}, f32[3,1,160,128]{3,2,0,1:T(8,128)}, u32[]{:S(2)}) copy-start(f32[3,1,160,128]{3,2,0,1:T(8,128)} %slice.254) | copy-start | bytes 737284
  60.0 7.2 %copy-start.14 = (f32[3,1,160,128]{3,2,0,1:T(8,128)S(1)}, f32[3,1,160,128]{3,2,0,1:T(8,128)}, u32[]{:S(2)}) copy-start(f32[3,1,160,128]{3,2,0,1:T(8,128)} %slice.255) | copy-start | bytes 737284
  61.7 5.6 %copy-start.13 = (f32[3,1,160,128]{3,2,0,1:T(8,128)S(1)}, f32[3,1,160,128]{3,2,0,1:T(8,128)}, u32[]{:S(2)}) copy-start(f32[3,1,160,128]{3,2,0,1:T(8,128)} %slice.256) | copy-start | bytes 737284
  65.0 2.3 %copy-start.12 = (f32[3,1,160,128]{3,2,0,1:T(8,128)S(1)}, f32[3,1,160,128]{3,2,0,1:T(8,128)}, u32[]{:S(2)}) copy-start(f32[3,1,160,128]{3,2,0,1:T(8,128)} %slice.257) | copy-start | bytes 737284
  65.7 1.7 copy-start.11
  67.3 1.3 copy-start.7
  67.3 2.0 %copy-start.6 = (f32[4,1,160,128]{3,2,0,1:T(8,128)S(1)}, f32[4,1,160,128]{3,2,0,1:T(8,128)}, u32[]{:S(2)}) copy-start(f32[4,1,160,128]{3,2,0,1:T(8,128)} %slice.272) | copy-start | bytes 983044
  68.1 2.0 %copy-start.5 = (f32[4,1,160,128]{3,2,0,1:T(8,128)S(1)}, f32[4,1,160,128]{3,2,0,1:T(8,128)}, u32[]{:S(2)}) copy-start(f32[4,1,160,128]{3,2,0,1:T(8,128)} %slice.273) | copy-start | bytes 983044
  68.2 2.6 %copy-start.4 = (f32[4,1,160,128]{3,2,0,1:T(8,128)S(1)}, f32[4,1,160,128]{3,2,0,1:T(8,128)}, u32[]{:S(2)}) copy-start(f32[4,1,160,128]{3,2,0,1:T(8,128)} %slice.274) | copy-start | bytes 983044
  68.4 3.3 %copy-start.3 = (f32[4,1,160,128]{3,2,0,1:T(8,128)S(1)}, f32[4,1,160,128]{3,2,0,1:T(8,128)}, u32[]{:S(2)}) copy-start(f32[4,1,160,128]{3,2,0,1:T(8,128)} %slice.275) | copy-start | bytes 983044
  94.4 4.0 %copy-start.2 = (bf16[1,1,160,512]{3,2,1,0:T(8,128)(2,1)S(1)}, bf16[1,1,160,512]{3,2,1,0:T(8,128)(2,1)}, u32[]{:S(2)}) copy-start(bf16[1,1,160,512]{3,2,1,0:T(8,128)(2,1)} %param.5) | copy-start | bytes 491524
  98.5 45.1 %copy-start.20 = (f32[512]{0:T(512)S(1)}, f32[512]{0:T(512)}, u32[]{:S(2)}) copy-start(f32[512]{0:T(512)} %param.6) | copy-start | bytes 6148
  98.5 45.1 %copy-start.21 = (f32[512]{0:T(512)S(1)}, f32[512]{0:T(512)}, u32[]{:S(2)}) copy-start(f32[512]{0:T(512)} %param.7) | copy-start | bytes 6148
  (3 other events, 3.1 us)
Sparse Core Ops, SparseCore 0:
  30.2 44.1 all-gather.1
  98.6 33.3 reduce-scatter.6

commit v2 on v1

--- a/solution.py
+++ b/solution.py
@@ -1,6 +1,10 @@
+import functools
+
 import jax
 import jax.numpy as jnp
 from jax import lax
+from jax.experimental import pallas as pl
+from jax.experimental.pallas import tpu as pltpu
 from jax.sharding import PartitionSpec as P
 
 GROUPS = 32
@@ -97,6 +101,418 @@
     return (latent_grad, gain_grad, bias_grad)
 
 
+MESH = pl.DeviceIdType.MESH
+
+
+def group_totals(value, member):
+    first = value.astype(jnp.bfloat16).astype(jnp.float32)
+    rest = value - first
+    second = rest.astype(jnp.bfloat16).astype(jnp.float32)
+    third = rest - second
+    parts = jnp.concatenate([first, second, third, jnp.zeros_like(first)], axis=0)
+    sums = jnp.dot(parts.astype(jnp.bfloat16), member, preferred_element_type=jnp.float32)
+    rows = value.shape[0]
+    return sums[:rows] + sums[rows : 2 * rows] + sums[2 * rows : 3 * rows]
+
+
+def fused_kernel(
+    frames, count, per_group, cells,
+    ct, w, lat, gain, bias,
+    out, gain_out, bias_out,
+    fine, wbuf, wcat, stack, pad, part, inbox, normed, slope, chan, member, st_rows, st_tm,
+    local_sem, ct_send, ct_recv, rim_send, rim_recv, z_send, z_recv, sib_send, sib_recv,
+    part_send, part_recv, sr_send, sr_recv, st_send, st_recv,
+):
+    chips = count // 2
+    low_cols, channels = lat.shape
+    fine_cols = ct.shape[1]
+    width = w.shape[2]
+    half = w.shape[1]
+    me_t = lax.axis_index("tm")
+    me_r = lax.axis_index("rows")
+    z = lax.div(me_r, 2)
+    core = lax.rem(me_r, 2)
+    sibling = me_r + 1 - 2 * core
+
+    def remote(src, dst, send, recv, t, r):
+        return pltpu.make_async_remote_copy(
+            src_ref=src, dst_ref=dst, send_sem=send, recv_sem=recv,
+            device_id=(t, r), device_id_type=MESH,
+        )
+
+    def frame_at(d):
+        return lax.rem(me_t + d, frames)
+
+    def row_at(d):
+        return lax.rem(me_r + d, count)
+
+    def lanes(t):
+        return pl.ds(pl.multiple_of(t * width, width), width)
+
+    def ct_copy(d):
+        t = frame_at(d)
+        return remote(
+            ct.at[:, :, lanes(t)], fine.at[me_t, pl.ds(1, 2)],
+            ct_send.at[d - 1], ct_recv.at[d - 1], t, me_r,
+        )
+
+    def rim_copy(side):
+        return remote(
+            fine.at[:, 1 + side], fine.at[:, 3 - 3 * side],
+            rim_send.at[side], rim_recv.at[side], me_t, row_at(count - 1 + 2 * side),
+        )
+
+    def z_copy(side, step, chip, first):
+        src = w if first else wbuf.at[chip, core]
+        to = row_at(2 if side == 0 else count - 2)
+        return remote(
+            src, wbuf.at[chip, core], z_send.at[side, step - 1], z_recv.at[side, step - 1],
+            me_t, to,
+        )
+
+    def sib_copy(chip, first):
+        src = w if first else wbuf.at[chip, core]
+        return remote(
+            src, wbuf.at[chip, core], sib_send.at[chip], sib_recv.at[chip], me_t, sibling
+        )
+
+    def part_copy(chip, d):
+        t = frame_at(d)
+        return remote(
+            part.at[chip, t], inbox.at[chip, d - 1],
+            part_send.at[chip, d - 1], part_recv.at[chip, d - 1], t, me_r,
+        )
+
+    def rows_copy(turn, d):
+        return remote(
+            st_rows.at[turn, me_r], st_rows.at[turn, me_r],
+            sr_send.at[turn, d - 1], sr_recv.at[turn, d - 1], me_t, row_at(d),
+        )
+
+    def tm_copy(turn, d):
+        return remote(
+            st_tm.at[turn, me_t], st_tm.at[turn, me_t],
+            st_send.at[turn, d - 1], st_recv.at[turn, d - 1], frame_at(d), me_r,
+        )
+
+    def rows_start(turn, first, second):
+        blank = jnp.zeros((6, channels), jnp.float32)
+        st_rows[turn, me_r] = jnp.concatenate([first, second, blank], axis=0)
+        for d in range(1, count):
+            rows_copy(turn, d).start()
+
+    def tm_start(turn):
+        for d in range(1, count):
+            rows_copy(turn, d).wait_recv()
+        total = st_rows[turn, 0]
+        for r in range(1, count):
+            total = total + st_rows[turn, r]
+        st_tm[turn, me_t] = total
+        for d in range(1, frames):
+            tm_copy(turn, d).start()
+
+    def tm_finish(turn):
+        for d in range(1, frames):
+            tm_copy(turn, d).wait_recv()
+        total = st_tm[turn, 0]
+        for t in range(1, frames):
+            total = total + st_tm[turn, t]
+        return total
+
+    barrier = pltpu.get_barrier_semaphore()
+    for d in range(1, count):
+        pl.semaphore_signal(barrier, inc=1, device_id=(me_t, row_at(d)), device_id_type=MESH)
+    for d in range(1, frames):
+        pl.semaphore_signal(barrier, inc=1, device_id=(frame_at(d), me_r), device_id_type=MESH)
+    pl.semaphore_wait(barrier, count + frames - 2)
+
+    for side in range(2):
+        to_chip = z + (1 if side == 0 else -1)
+
+        @pl.when((to_chip >= 0) & (to_chip < chips))
+        def _():
+            z_copy(side, 1, z, True).start()
+
+    for d in range(1, frames):
+        ct_copy(d).start()
+    sib_copy(z, True).start()
+    own_ct = pltpu.make_async_copy(
+        ct.at[:, :, lanes(me_t)], fine.at[me_t, pl.ds(1, 2)], local_sem.at[0]
+    )
+    own_w = pltpu.make_async_copy(w, wbuf.at[z, core], local_sem.at[1])
+    own_ct.start()
+    own_w.start()
+
+    features = lat[...].astype(jnp.float32)
+    rows_start(
+        0,
+        jnp.sum(features, axis=0, keepdims=True),
+        jnp.sum(features * features, axis=0, keepdims=True),
+    )
+    shift = per_group.bit_length() - 1
+    left = lax.shift_right_logical(lax.broadcasted_iota(jnp.int32, (channels, channels), 0), shift)
+    right = lax.shift_right_logical(lax.broadcasted_iota(jnp.int32, (channels, channels), 1), shift)
+    member[...] = jnp.where(left == right, 1.0, 0.0).astype(jnp.bfloat16)
+    edge = jnp.zeros((8, width), jnp.float32)
+    for u in range(6):
+        pad[u, 0:8] = edge
+        pad[u, fine_cols + 8 : fine_cols + 16] = edge
+
+    @pl.when(me_r == 0)
+    def _():
+        fine[:, 0] = jnp.zeros((frames, fine_cols, width), jnp.bfloat16)
+
+    @pl.when(me_r == count - 1)
+    def _():
+        fine[:, 3] = jnp.zeros((frames, fine_cols, width), jnp.bfloat16)
+
+    own_ct.wait()
+    for d in range(1, frames):
+        ct_copy(d).wait_recv()
+
+    @pl.when(me_r > 0)
+    def _():
+        rim_copy(0).start()
+
+    @pl.when(me_r < count - 1)
+    def _():
+        rim_copy(1).start()
+
+    tm_start(0)
+    own_w.wait()
+
+    def arrive(step):
+        for side in range(2):
+            sign = 1 if side == 0 else -1
+            chip = z - sign * step
+            to_chip = z + sign
+
+            @pl.when((chip >= 0) & (chip < chips))
+            def _():
+                z_copy(side, step, chip, False).wait_recv()
+
+                @pl.when((to_chip >= 0) & (to_chip < chips))
+                def _():
+                    z_copy(side, step + 1, chip, False).start()
+
+                sib_copy(chip, False).start()
+
+    def prepare():
+        @pl.when(me_r < count - 1)
+        def _():
+            rim_copy(0).wait_recv()
+
+        @pl.when(me_r > 0)
+        def _():
+            rim_copy(1).wait_recv()
+
+        for b in range(3):
+            rows = [
+                fine[t, 2 - b].astype(jnp.float32) + fine[t, 3 - b].astype(jnp.float32)
+                for t in range(frames)
+            ]
+            early = rows[0] + rows[1]
+            for u, value in enumerate(rows + [early, early + rows[2]]):
+                pad[u, 8 : fine_cols + 8] = value
+            for u in range(6):
+                lines = [pad[u, pl.ds(7 + k, low_cols, stride=2), :] for k in range(4)]
+                for c in range(3):
+                    box = lines[2 - c] + lines[3 - c]
+                    high = box.astype(jnp.bfloat16)
+                    low = (box - high.astype(jnp.float32)).astype(jnp.bfloat16)
+                    tap = slice((3 * b + c) * width, (3 * b + c + 1) * width)
+                    stack[u, 0:low_cols, tap] = high
+                    stack[u, low_cols : 2 * low_cols, tap] = low
+
+        totals = tm_finish(0)
+        scale = 1.0 / (cells * per_group)
+        means = group_totals(totals, member[...]) * scale
+        mean = means[0:1]
+        inv = lax.rsqrt(means[1:2] - mean * mean + 1e-06)
+        chan[0:1] = inv
+        centred = (lat[...].astype(jnp.float32) - mean) * inv
+        normed[...] = centred
+        pre = centred * gain[...] + bias[...]
+        sg = 1.0 / (1.0 + jnp.exp(-pre))
+        slope[...] = sg * (1.0 + pre * (1.0 - sg))
+
+    def process(chip):
+        sib_copy(chip, False).wait_recv()
+        for a in range(3):
+            for k in range(9):
+                for side in range(2):
+                    wcat[a, side * half : (side + 1) * half, k * width : (k + 1) * width] = wbuf[
+                        chip, side, 9 * a + k
+                    ]
+        for t in range(frames):
+            total = None
+            for a, u in (((2, 0), (1, 4), (0, 5)) if t == 0 else zip((2, 1, 0), range(t, frames))):
+                product = lax.dot_general(
+                    stack[u], wcat[a], (((1,), (1,)), ((), ())), preferred_element_type=jnp.float32
+                )
+                total = product if total is None else total + product
+            part[chip, t] = total[:low_cols] + total[low_cols:]
+        for d in range(1, frames):
+            part_copy(chip, d).start()
+
+    def turn(k, carry):
+        @pl.when(k + 1 < chips)
+        def _():
+            arrive(k + 1)
+
+        @pl.when(k == 0)
+        def _():
+            prepare()
+
+        def one_side(side, inner):
+            chip = z + (2 * side - 1) * k
+
+            @pl.when((chip >= 0) & (chip < chips) & ((k > 0) | (side == 0)))
+            def _():
+                process(chip)
+
+            return inner
+
+        return lax.fori_loop(0, 2, one_side, carry)
+
+    lax.fori_loop(0, chips, turn, 0)
+
+    sums, scaled_sums = [], []
+    for chip in range(chips):
+        span = slice(2 * half * chip, 2 * half * (chip + 1))
+        up = part[chip, me_t]
+        for d in range(1, frames):
+            part_copy(chip, d).wait_recv()
+            up = up + inbox[chip, d - 1]
+        act = up * slope[:, span]
+        out[:, span] = act
+        sums.append(jnp.sum(act, axis=0, keepdims=True))
+        scaled_sums.append(jnp.sum(act * normed[:, span], axis=0, keepdims=True))
+    rows_start(1, jnp.concatenate(sums, axis=1), jnp.concatenate(scaled_sums, axis=1))
+    tm_start(1)
+    totals = tm_finish(1)
+    bias_out[...] = totals[0:1] * (1.0 / cells)
+    gain_out[...] = totals[1:2] * (1.0 / cells)
+    means = group_totals(totals * gain[...], member[...]) * (1.0 / (cells * per_group))
+    inv = chan[0:1]
+    out[...] = inv * (out[...] * gain[...] - means[0:1] - normed[...] * means[1:2])
+
+    for d in range(1, frames):
+        ct_copy(d).wait_send()
+        for chip in range(chips):
+            part_copy(chip, d).wait_send()
+        for turn_index in range(2):
+            tm_copy(turn_index, d).wait_send()
+    for d in range(1, count):
+        for turn_index in range(2):
+            rows_copy(turn_index, d).wait_send()
+
+    @pl.when(me_r > 0)
+    def _():
+        rim_copy(0).wait_send()
+
+    @pl.when(me_r < count - 1)
+    def _():
+        rim_copy(1).wait_send()
+
+    for chip in range(chips):
+        sib_copy(chip, False).wait_send()
+    for side in range(2):
+        sign = 1 if side == 0 else -1
+        to_chip = z + sign
+        for step in range(1, chips):
+            chip = z - sign * (step - 1)
+
+            @pl.when((to_chip >= 0) & (to_chip < chips) & (chip >= 0) & (chip < chips))
+            def _():
+                z_copy(side, step, chip, False).wait_send()
+
+
+def fused(latent, norm_gain, norm_bias, conv_weight, cotangent):
+    frames = lax.axis_size("tm")
+    count = lax.axis_size("rows")
+    low_cols, channels = latent.shape[2:]
+    fine_cols = cotangent.shape[2]
+    half, width = conv_weight.shape[3:]
+    chips = count // 2
+    f32, bf16 = jnp.float32, jnp.bfloat16
+    dma = pltpu.SemaphoreType.DMA
+    body = functools.partial(
+        fused_kernel, frames, count, channels // GROUPS, frames * count * low_cols
+    )
+    vmem = pl.BlockSpec(memory_space=pltpu.VMEM)
+    products = chips * 9 * 2 * low_cols * 9 * width * 2 * half
+    grad, gain_grad, bias_grad = pl.pallas_call(
+        body,
+        out_shape=(
+            jax.ShapeDtypeStruct((low_cols, channels), f32),
+            jax.ShapeDtypeStruct((1, channels), f32),
+            jax.ShapeDtypeStruct((1, channels), f32),
+        ),
+        in_specs=[vmem] * 5,
+        out_specs=(vmem,) * 3,
+        scratch_shapes=[
+            pltpu.VMEM((frames, 4, fine_cols, width), bf16),
+            pltpu.VMEM((chips, 2, 27, half, width), bf16),
+            pltpu.VMEM((3, 2 * half, 9 * width), bf16),
+            pltpu.VMEM((6, 2 * low_cols, 9 * width), bf16),
+            pltpu.VMEM((6, fine_cols + 16, width), f32),
+            pltpu.VMEM((chips, frames, low_cols, 2 * half), f32),
+            pltpu.VMEM((chips, frames - 1, low_cols, 2 * half), f32),
+            pltpu.VMEM((low_cols, channels), f32),
+            pltpu.VMEM((low_cols, channels), f32),
+            pltpu.VMEM((8, channels), f32),
+            pltpu.VMEM((channels, channels), bf16),
+            pltpu.VMEM((2, count, 8, channels), f32),
+            pltpu.VMEM((2, frames, 8, channels), f32),
+            dma((2,)),
+            dma((frames - 1,)),
+            dma((frames - 1,)),
+            dma((2,)),
+            dma((2,)),
+            dma((2, chips)),
+            dma((2, chips)),
+            dma((chips,)),
+            dma((chips,)),
+            dma((chips, frames - 1)),
+            dma((chips, frames - 1)),
+            dma((2, count - 1)),
+            dma((2, count - 1)),
+            dma((2, frames - 1)),
+            dma((2, frames - 1)),
+        ],
+        compiler_params=pltpu.CompilerParams(
+            collective_id=0, has_side_effects=True, vmem_limit_bytes=48 * 1024 * 1024
+        ),
+        cost_estimate=pl.CostEstimate(
+            flops=2 * products, bytes_accessed=2 * 1024 * 1024, transcendentals=low_cols * channels
+        ),
+    )(
+        cotangent.reshape(cotangent.shape[1:]),
+        conv_weight.reshape((27, half, width)),
+        latent.reshape((low_cols, channels)),
+        norm_gain.reshape((1, channels)),
+        norm_bias.reshape((1, channels)),
+    )
+    return grad.reshape(latent.shape), gain_grad.reshape(-1), bias_grad.reshape(-1)
+
+
+def on_device(latent, norm_gain, norm_bias, conv_weight, cotangent):
+    half, width = conv_weight.shape[3:]
+    per_group = latent.shape[3] // GROUPS
+    fits = (
+        lax.axis_size("tm") == 4
+        and latent.shape[1] == 1
+        and lax.axis_size("rows") % 2 == 0
+        and half % 64 == 0
+        and width % 128 == 0
+        and latent.shape[2] % 16 == 0
+        and per_group & (per_group - 1) == 0
+    )
+    run = fused if fits else spread_out
+    return run(latent, norm_gain, norm_bias, conv_weight, cotangent)
+
+
 def solution(mesh):
     placed = (
         P("tm", "rows", None, None),
@@ -106,7 +522,7 @@
         P("tm", "rows", None, None),
     )
     return jax.shard_map(
-        spread_out,
+        on_device,
         mesh=mesh,
         in_specs=placed,
         out_specs=(P("tm", "rows", None, None), P(), P()),

time: 194 us -> 68.8 us (0.35)
  blocking collectives: 100 us -> 0 us
  Pallas kernels: 0 us -> 62.3 us
  local copies, waits for them, and re-layouts: 53.4 us -> 5.58 us
  between operations: 14.5 us -> 0.66 us
  matrix products: 12.6 us -> 0 us
  other arithmetic: 6.04 us -> 0 us
  waiting for transfers between devices: 3.97 us -> 0 us
  starting transfers between devices: 2.68 us -> 0 us
    psum x2 -> x0, blocking collectives: 83.9 us -> none  [the longest x1 44.3 us: spread_out(): total_x, total_sq = lax.psum((sum_x, sum_sq), ('tm', 'rows'))]
    pallas_call x0 -> x1, Pallas kernels: none -> 62.3 us  [fused(): pl.pallas_call(body, out_shape=(jax.ShapeDtypeStruct((low_cols, channels)...]
    unnamed x77 -> x13, local copies, waits for them, and re-layouts: 30 us -> 5.58 us
    slice x30 -> x0, local copies, waits for them, and re-layouts: 18.6 us -> none  [the longest x27 18.1 us: up_grad_part(): stack[:, 2 - b:1 - b + 2 * low_rows:2, 2 - c:1 - c + 2 * low_cols:2]]
    all_to_all x1 -> x0, blocking collectives: 16.3 us -> none  [spread_out(): lax.all_to_all(cotangent, 'tm', split_axis=3, concat_axis=0, tiled=True)]
    dot_general x6 -> x0, matrix products: 12.6 us -> none  [up_grad_part(): lax.dot_general(part, kernel, (((3,), (1,)), ((), ())), preferred_element...]
    ppermute x2 -> x0, waiting for transfers between devices: 3.93 us -> none  [the longest x1 3.93 us: row_rims(): high = lax.ppermute(block[:, :1], 'rows', backward)]
    concatenate x4 -> x0, local copies, waits for them, and re-layouts: 2.65 us -> none  [the longest x3 1.52 us: up_grad_part(): wide = jnp.concatenate(taps, axis=-1)]
  transfers between devices with their start and end apart: 4 -> 0, of which waited for: 1 -> 0; matrix products, arithmetic and copies ran while one was open for 21% -> 0% of each run, Pallas kernels for 0% -> 0%
where the time goes in v2:
time: 68.8 us; the launch traced here: 68.6 us
  Pallas kernels  62.3 us (91%)
  local copies, waits for them, and re-layouts  5.58 us (8%)
    pallas_call x1, Pallas kernels, fused(): pl.pallas_call(body, out_shape=(jax.ShapeDtypeStruct((low_cols, channels)...  62.3 us
    unnamed x13, local copies, waits for them, and re-layouts  5.58 us

profile of v2, /device:TPU:0, one launch (start us, length us, event | category | flops | bytes accessed | tf_op | source)
XLA Modules:
  0.0 68.6 jit_solution(5319275568805324090)
XLA Ops:
  0.6 0.0 copy-start.4
  0.6 0.0 copy-start.3
  0.7 0.7 copy-done.4
  1.3 0.0 copy-done.3
  1.3 0.0 copy-start
  1.3 1.1 %copy-done = bf16[1,2,320,512]{3,2,1,0:T(8,128)(2,1)S(1)} copy-done((bf16[1,2,320,512]{3,2,1,0:T(8,128)(2,1)S(1)}, bf16[1,2,320,512]{3,2,1,0:T(8,128)(2,1)}, u32[]{:S(2)}) %copy-start) | copy-done | bytes 655384
  2.4 0.0 copy-start.1
  2.4 1.0 %copy-done.1 = bf16[3,3,3,64,128]{4,3,2,1,0:T(8,128)(2,1)S(1)} copy-done((bf16[3,3,3,64,128]{4,3,2,1,0:T(8,128)(2,1)S(1)}, bf16[3,3,3,64,128]{4,3,2,1,0:T(8,128)(2,1)}, u32[]{:S(2)}) %copy-start.1) | copy-done | bytes 442392
  3.4 0.0 copy-start.2
  3.4 0.9 %copy-done.2 = bf16[1,1,160,512]{3,2,1,0:T(8,128)(2,1)S(1)} copy-done((bf16[1,1,160,512]{3,2,1,0:T(8,128)(2,1)S(1)}, bf16[1,1,160,512]{3,2,1,0:T(8,128)(2,1)}, u32[]{:S(2)}) %copy-start.2) | copy-done | bytes 163864
  4.3 62.3 %shard_map.76 = (f32[160,512]{1,0:T(8,128)S(1)}, f32[1,512]{1,0:T(1,128)S(1)}, f32[1,512]{1,0:T(1,128)S(1)}) custom-call(bf16[2,320,512]{2,1,0:T(8,128)(2,1)S(1)} %bitcast.11, bf16[27,64,128]{2,1,0:T(8,128)(2,1)S(1)} %bitcast.12, bf16[160,512]{1,0:T(8,128)(2,1)S(1)} %bitcast.13, f32[1,512]{1,0:T(1,128)S(1)} %bitcast.14, f32[1,512]{1,0:T(1,128)S(1)} %bitcast.15), custom_call_target="tpu_custom_call" | custom-call | flops 3397386240 | bytes 2097152 | tf_op jit(solution)/shard_map/pallas_call | solution.py:445
  66.7 0.7 %copy.11 = f32[1,1,160,512]{3,2,1,0:T(8,128)} copy(f32[1,1,160,512]{3,2,1,0:T(8,128)S(1)} %bitcast.8) | data formatting | bytes 655360
  67.4 0.6 copy.12
  68.0 0.6 copy.13
Async XLA Ops:
  0.6 0.7 copy-start.4
  0.6 0.7 %copy-start.3 = (f32[512]{0:T(512)S(1)}, f32[512]{0:T(512)}, u32[]{:S(2)}) copy-start(f32[512]{0:T(512)} %param.6) | copy-start | bytes 6148
  1.3 1.1 %copy-start = (bf16[1,2,320,512]{3,2,1,0:T(8,128)(2,1)S(1)}, bf16[1,2,320,512]{3,2,1,0:T(8,128)(2,1)}, u32[]{:S(2)}) copy-start(bf16[1,2,320,512]{3,2,1,0:T(8,128)(2,1)} %param.9) | copy-start | bytes 1966084
  2.4 1.0 %copy-start.1 = (bf16[3,3,3,64,128]{4,3,2,1,0:T(8,128)(2,1)S(1)}, bf16[3,3,3,64,128]{4,3,2,1,0:T(8,128)(2,1)}, u32[]{:S(2)}) copy-start(bf16[3,3,3,64,128]{4,3,2,1,0:T(8,128)(2,1)} %param.8) | copy-start | bytes 1327108
  3.4 0.9 %copy-start.2 = (bf16[1,1,160,512]{3,2,1,0:T(8,128)(2,1)S(1)}, bf16[1,1,160,512]{3,2,1,0:T(8,128)(2,1)}, u32[]{:S(2)}) copy-start(bf16[1,1,160,512]{3,2,1,0:T(8,128)(2,1)} %param.5) | copy-start | bytes 491524

commit v3 on v2

--- a/solution.py
+++ b/solution.py
@@ -117,9 +117,9 @@
 
 def fused_kernel(
     frames, count, per_group, cells,
-    ct, w, lat, gain, bias,
+    ct, w, lat_hbm, gain_hbm, bias_hbm,
     out, gain_out, bias_out,
-    fine, wbuf, wcat, stack, pad, part, inbox, normed, slope, chan, member, st_rows, st_tm,
+    lat, gain, bias, acc, fine, wbuf, wcat, stack, pad, part, inbox, normed, slope, chan, member, st_rows, st_tm,
     local_sem, ct_send, ct_recv, rim_send, rim_recv, z_send, z_recv, sib_send, sib_recv,
     part_send, part_recv, sr_send, sr_recv, st_send, st_recv,
 ):
@@ -162,18 +162,20 @@
             rim_send.at[side], rim_recv.at[side], me_t, row_at(count - 1 + 2 * side),
         )
 
-    def z_copy(side, step, chip, first):
-        src = w if first else wbuf.at[chip, core]
-        to = row_at(2 if side == 0 else count - 2)
-        return remote(
-            src, wbuf.at[chip, core], z_send.at[side, step - 1], z_recv.at[side, step - 1],
-            me_t, to,
-        )
-
-    def sib_copy(chip, first):
-        src = w if first else wbuf.at[chip, core]
-        return remote(
-            src, wbuf.at[chip, core], sib_send.at[chip], sib_recv.at[chip], me_t, sibling
+    def piece(chip, a):
+        return wbuf.at[chip, core, pl.ds(9 * a, 9)]
+
+    def z_copy(side, step, chip, a, first):
+        return remote(
+            w.at[pl.ds(9 * a, 9)] if first else piece(chip, a), piece(chip, a),
+            z_send.at[side, step - 1, a], z_recv.at[side, step - 1, a],
+            me_t, row_at(2 + side * (count - 4)),
+        )
+
+    def sib_copy(chip, a, first):
+        return remote(
+            w.at[pl.ds(9 * a, 9)] if first else piece(chip, a), piece(chip, a),
+            sib_send.at[chip, a], sib_recv.at[chip, a], me_t, sibling,
         )
 
     def part_copy(chip, d):
@@ -196,8 +198,10 @@
         )
 
     def rows_start(turn, first, second):
-        blank = jnp.zeros((6, channels), jnp.float32)
-        st_rows[turn, me_r] = jnp.concatenate([first, second, blank], axis=0)
+        st_rows[turn, me_r] = jnp.concatenate(
+            [line[:, k : k + 128] for line in (first, second) for k in range(0, channels, 128)],
+            axis=0,
+        )
         for d in range(1, count):
             rows_copy(turn, d).start()
 
@@ -217,8 +221,27 @@
         total = st_tm[turn, 0]
         for t in range(1, frames):
             total = total + st_tm[turn, t]
-        return total
-
+        lines = channels // 128
+        first, second = (
+            jnp.concatenate([total[k : k + 1] for k in range(start, start + lines)], axis=1)
+            for start in (0, lines)
+        )
+        return jnp.concatenate([first, second, jnp.zeros((6, channels), jnp.float32)], axis=0)
+
+    own = [
+        pltpu.make_async_copy(src, dst, local_sem.at[k])
+        for k, (src, dst) in enumerate(
+            [
+                (lat_hbm, lat),
+                (gain_hbm, gain),
+                (bias_hbm, bias),
+                (ct.at[:, :, lanes(me_t)], fine.at[me_t, pl.ds(1, 2)]),
+                (w, wbuf.at[z, core]),
+            ]
+        )
+    ]
+    for copy in own:
+        copy.start()
     barrier = pltpu.get_barrier_semaphore()
     for d in range(1, count):
         pl.semaphore_signal(barrier, inc=1, device_id=(me_t, row_at(d)), device_id_type=MESH)
@@ -231,18 +254,16 @@
 
         @pl.when((to_chip >= 0) & (to_chip < chips))
         def _():
-            z_copy(side, 1, z, True).start()
+            for a in (2, 1, 0):
+                z_copy(side, 1, z, a, True).start()
 
     for d in range(1, frames):
         ct_copy(d).start()
-    sib_copy(z, True).start()
-    own_ct = pltpu.make_async_copy(
-        ct.at[:, :, lanes(me_t)], fine.at[me_t, pl.ds(1, 2)], local_sem.at[0]
-    )
-    own_w = pltpu.make_async_copy(w, wbuf.at[z, core], local_sem.at[1])
-    own_ct.start()
-    own_w.start()
-
+    for a in (2, 1, 0):
+        sib_copy(z, a, True).start()
+
+    for copy in own[:3]:
+        copy.wait()
     features = lat[...].astype(jnp.float32)
     rows_start(
         0,
@@ -266,7 +287,7 @@
     def _():
         fine[:, 3] = jnp.zeros((frames, fine_cols, width), jnp.bfloat16)
 
-    own_ct.wait()
+    own[3].wait()
     for d in range(1, frames):
         ct_copy(d).wait_recv()
 
@@ -279,23 +300,24 @@
         rim_copy(1).start()
 
     tm_start(0)
-    own_w.wait()
+    own[4].wait()
 
     def arrive(step):
-        for side in range(2):
-            sign = 1 if side == 0 else -1
-            chip = z - sign * step
-            to_chip = z + sign
-
-            @pl.when((chip >= 0) & (chip < chips))
-            def _():
-                z_copy(side, step, chip, False).wait_recv()
-
-                @pl.when((to_chip >= 0) & (to_chip < chips))
+        for a in (2, 1, 0):
+            for side in range(2):
+                sign = 1 if side == 0 else -1
+                chip = z - sign * step
+                to_chip = z + sign
+
+                @pl.when((chip >= 0) & (chip < chips))
                 def _():
-                    z_copy(side, step + 1, chip, False).start()
-
-                sib_copy(chip, False).start()
+                    z_copy(side, step, chip, a, False).wait_recv()
+
+                    @pl.when((to_chip >= 0) & (to_chip < chips))
+                    def _():
+                        z_copy(side, step + 1, chip, a, False).start()
+
+                    sib_copy(chip, a, False).start()
 
     def prepare():
         @pl.when(me_r < count - 1)
@@ -336,27 +358,39 @@
         sg = 1.0 / (1.0 + jnp.exp(-pre))
         slope[...] = sg * (1.0 + pre * (1.0 - sg))
 
-    def process(chip):
-        sib_copy(chip, False).wait_recv()
-        for a in range(3):
-            for k in range(9):
-                for side in range(2):
-                    wcat[a, side * half : (side + 1) * half, k * width : (k + 1) * width] = wbuf[
-                        chip, side, 9 * a + k
-                    ]
-        for t in range(frames):
-            total = None
-            for a, u in (((2, 0), (1, 4), (0, 5)) if t == 0 else zip((2, 1, 0), range(t, frames))):
-                product = lax.dot_general(
-                    stack[u], wcat[a], (((1,), (1,)), ((), ())), preferred_element_type=jnp.float32
+    def process(chip, side, k):
+        for a in (2, 1, 0):
+
+            @pl.when(k == chips - 1)
+            def _():
+                z_copy(side, chips - 1, chip, a, False).wait_recv()
+                sib_copy(chip, a, False).start()
+
+            sib_copy(chip, a, False).wait_recv()
+            for tap in range(9):
+                for part_of in range(2):
+                    wcat[
+                        a, part_of * half : (part_of + 1) * half, tap * width : (tap + 1) * width
+                    ] = wbuf[chip, part_of, 9 * a + tap]
+            for t in range(min(frames, a + 2) - 1, -1, -1):
+                unit = (5, 4, 0)[a] if t == 0 else t + 2 - a
+                total = lax.dot_general(
+                    stack[unit], wcat[a], (((1,), (1,)), ((), ())),
+                    preferred_element_type=jnp.float32,
                 )
-                total = product if total is None else total + product
-            part[chip, t] = total[:low_cols] + total[low_cols:]
-        for d in range(1, frames):
-            part_copy(chip, d).start()
+                if a < 2:
+                    total = total + acc[t]
+                if a > max(0, t - 1):
+                    acc[t] = total
+                    continue
+                part[chip, t] = total[:low_cols] + total[low_cols:]
+
+                @pl.when(me_t != t)
+                def _():
+                    part_copy(chip, lax.rem(t - me_t + frames, frames)).start()
 
     def turn(k, carry):
-        @pl.when(k + 1 < chips)
+        @pl.when(k + 1 < chips - 1)
         def _():
             arrive(k + 1)
 
@@ -369,7 +403,7 @@
 
             @pl.when((chip >= 0) & (chip < chips) & ((k > 0) | (side == 0)))
             def _():
-                process(chip)
+                process(chip, side, k)
 
             return inner
 
@@ -416,7 +450,8 @@
         rim_copy(1).wait_send()
 
     for chip in range(chips):
-        sib_copy(chip, False).wait_send()
+        for a in range(3):
+            sib_copy(chip, a, False).wait_send()
     for side in range(2):
         sign = 1 if side == 0 else -1
         to_chip = z + sign
@@ -425,7 +460,8 @@
 
             @pl.when((to_chip >= 0) & (to_chip < chips) & (chip >= 0) & (chip < chips))
             def _():
-                z_copy(side, step, chip, False).wait_send()
+                for a in range(3):
+                    z_copy(side, step, chip, a, False).wait_send()
 
 
 def fused(latent, norm_gain, norm_bias, conv_weight, cotangent):
@@ -449,9 +485,13 @@
             jax.ShapeDtypeStruct((1, channels), f32),
             jax.ShapeDtypeStruct((1, channels), f32),
         ),
-        in_specs=[vmem] * 5,
+        in_specs=[pl.BlockSpec(memory_space=pltpu.HBM)] * 5,
         out_specs=(vmem,) * 3,
         scratch_shapes=[
+            pltpu.VMEM((low_cols, channels), bf16),
+            pltpu.VMEM((1, channels), f32),
+            pltpu.VMEM((1, channels), f32),
+            pltpu.VMEM((frames - 1, 2 * low_cols, 2 * half), f32),
             pltpu.VMEM((frames, 4, fine_cols, width), bf16),
             pltpu.VMEM((chips, 2, 27, half, width), bf16),
             pltpu.VMEM((3, 2 * half, 9 * width), bf16),
@@ -463,17 +503,17 @@
             pltpu.VMEM((low_cols, channels), f32),
             pltpu.VMEM((8, channels), f32),
             pltpu.VMEM((channels, channels), bf16),
-            pltpu.VMEM((2, count, 8, channels), f32),
-            pltpu.VMEM((2, frames, 8, channels), f32),
-            dma((2,)),
+            pltpu.VMEM((2, count, channels // 64, 128), f32),
+            pltpu.VMEM((2, frames, channels // 64, 128), f32),
+            dma((5,)),
             dma((frames - 1,)),
             dma((frames - 1,)),
             dma((2,)),
             dma((2,)),
-            dma((2, chips)),
-            dma((2, chips)),
-            dma((chips,)),
-            dma((chips,)),
+            dma((2, chips - 1, 3)),
+            dma((2, chips - 1, 3)),
+            dma((chips, 3)),
+            dma((chips, 3)),
             dma((chips, frames - 1)),
             dma((chips, frames - 1)),
             dma((2, count - 1)),
@@ -482,7 +522,7 @@
             dma((2, frames - 1)),
         ],
         compiler_params=pltpu.CompilerParams(
-            collective_id=0, has_side_effects=True, vmem_limit_bytes=48 * 1024 * 1024
+            collective_id=0, has_side_effects=True, vmem_limit_bytes=62 * 1024 * 1024
         ),
         cost_estimate=pl.CostEstimate(
             flops=2 * products, bytes_accessed=2 * 1024 * 1024, transcendentals=low_cols * channels
@@ -503,6 +543,7 @@
     fits = (
         lax.axis_size("tm") == 4
         and latent.shape[1] == 1
+        and latent.shape[3] % 512 == 0
         and lax.axis_size("rows") % 2 == 0
         and half % 64 == 0
         and width % 128 == 0

time: 68.8 us -> 61.3 us (0.89)
  Pallas kernels: 62.3 us -> 57.6 us
  local copies, waits for them, and re-layouts: 5.58 us -> 2.97 us
    pallas_call x1, Pallas kernels: 62.3 us -> 57.6 us  [fused(): pl.pallas_call(body, out_shape=(jax.ShapeDtypeStruct((low_cols, channels)...]
    unnamed x13 -> x7, local copies, waits for them, and re-layouts: 5.58 us -> 2.97 us
where the time goes in v3:
time: 61.3 us; the launch traced here: 61.2 us
  Pallas kernels  57.6 us (94%)
  local copies, waits for them, and re-layouts  2.97 us (5%)
  between operations  0.65 us (1%)
    pallas_call x1, Pallas kernels, fused(): pl.pallas_call(body, out_shape=(jax.ShapeDtypeStruct((low_cols, channels)...  57.6 us
    unnamed x7, local copies, waits for them, and re-layouts  2.97 us

profile of v3, /device:TPU:0, one launch (start us, length us, event | category | flops | bytes accessed | tf_op | source)
XLA Modules:
  0.0 61.2 jit_solution(10120976285264268395)
XLA Ops:
  0.6 57.6 %shard_map.76 = (f32[160,512]{1,0:T(8,128)}, f32[1,512]{1,0:T(1,128)}, f32[1,512]{1,0:T(1,128)}) custom-call(bf16[2,320,512]{2,1,0:T(8,128)(2,1)} %bitcast.11, bf16[27,64,128]{2,1,0:T(8,128)(2,1)} %bitcast.12, bf16[160,512]{1,0:T(8,128)(2,1)} %bitcast.13, f32[1,512]{1,0:T(1,128)} %bitcast.14, f32[1,512]{1,0:T(1,128)} %bitcast.15), custom_call_target="tpu_custom_call" | custom-call | flops 3397386240 | bytes 2097152 | tf_op jit(solution)/shard_map/pallas_call | solution.py:481
  58.2 0.0 copy-start.1
  58.2 1.7 %copy.11 = f32[1,1,160,512]{3,2,1,0:T(8,128)} copy(f32[1,1,160,512]{3,2,1,0:T(8,128)} %bitcast.8) | data formatting | bytes 655360
  59.9 0.0 copy-done.1
  59.9 0.0 copy-start
  59.9 0.6 copy.12
  60.5 0.1 copy-done
  60.6 0.6 copy.13
Async XLA Ops:
  58.2 1.7 %copy-start.1 = (f32[1,512]{1,0:T(1,128)S(1)}, f32[1,512]{1,0:T(1,128)}, u32[]{:S(2)}) copy-start(f32[1,512]{1,0:T(1,128)} %get-tuple-element.7) | copy-start | bytes 6148
  59.9 0.7 %copy-start = (f32[1,512]{1,0:T(1,128)S(1)}, f32[1,512]{1,0:T(1,128)}, u32[]{:S(2)}) copy-start(f32[1,512]{1,0:T(1,128)} %get-tuple-element.8) | copy-start | bytes 6148

commit v4 on v3

--- a/solution.py
+++ b/solution.py
@@ -343,8 +343,9 @@
                     high = box.astype(jnp.bfloat16)
                     low = (box - high.astype(jnp.float32)).astype(jnp.bfloat16)
                     tap = slice((3 * b + c) * width, (3 * b + c + 1) * width)
-                    stack[u, 0:low_cols, tap] = high
-                    stack[u, low_cols : 2 * low_cols, tap] = low
+                    for slot in ((0,), (1,), (2, 5), (3, 6, 8), (4,), (7,))[u]:
+                        stack[slot, 0:low_cols, tap] = high
+                        stack[slot, low_cols : 2 * low_cols, tap] = low
 
         totals = tm_finish(0)
         scale = 1.0 / (cells * per_group)
@@ -372,12 +373,15 @@
                     wcat[
                         a, part_of * half : (part_of + 1) * half, tap * width : (tap + 1) * width
                     ] = wbuf[chip, part_of, 9 * a + tap]
-            for t in range(min(frames, a + 2) - 1, -1, -1):
-                unit = (5, 4, 0)[a] if t == 0 else t + 2 - a
-                total = lax.dot_general(
-                    stack[unit], wcat[a], (((1,), (1,)), ((), ())),
-                    preferred_element_type=jnp.float32,
-                )
+            first_slot = (7, 4, 0)[a]
+            product = lax.dot_general(
+                stack[first_slot : first_slot + a + 2].reshape((a + 2) * 2 * low_cols, 9 * width),
+                wcat[a],
+                (((1,), (1,)), ((), ())),
+                preferred_element_type=jnp.float32,
+            )
+            for t in range(a + 1, -1, -1):
+                total = product[2 * low_cols * t : 2 * low_cols * (t + 1)]
                 if a < 2:
                     total = total + acc[t]
                 if a > max(0, t - 1):
@@ -481,9 +485,9 @@
     grad, gain_grad, bias_grad = pl.pallas_call(
         body,
         out_shape=(
-            jax.ShapeDtypeStruct((low_cols, channels), f32),
-            jax.ShapeDtypeStruct((1, channels), f32),
-            jax.ShapeDtypeStruct((1, channels), f32),
+            pltpu.VMEM((low_cols, channels), f32),
+            pltpu.VMEM((1, channels), f32),
+            pltpu.VMEM((1, channels), f32),
         ),
         in_specs=[pl.BlockSpec(memory_space=pltpu.HBM)] * 5,
         out_specs=(vmem,) * 3,
@@ -495,7 +499,7 @@
             pltpu.VMEM((frames, 4, fine_cols, width), bf16),
             pltpu.VMEM((chips, 2, 27, half, width), bf16),
             pltpu.VMEM((3, 2 * half, 9 * width), bf16),
-            pltpu.VMEM((6, 2 * low_cols, 9 * width), bf16),
+            pltpu.VMEM((9, 2 * low_cols, 9 * width), bf16),
             pltpu.VMEM((6, fine_cols + 16, width), f32),
             pltpu.VMEM((chips, frames, low_cols, 2 * half), f32),
             pltpu.VMEM((chips, frames - 1, low_cols, 2 * half), f32),
@@ -522,7 +526,7 @@
             dma((2, frames - 1)),
         ],
         compiler_params=pltpu.CompilerParams(
-            collective_id=0, has_side_effects=True, vmem_limit_bytes=62 * 1024 * 1024
+            collective_id=0, has_side_effects=True, vmem_limit_bytes=60 * 1024 * 1024
         ),
         cost_estimate=pl.CostEstimate(
             flops=2 * products, bytes_accessed=2 * 1024 * 1024, transcendentals=low_cols * channels

time: 61.3 us -> 60.6 us (0.989)
  local copies, waits for them, and re-layouts: 2.97 us -> 1.88 us
    unnamed x7 -> x3, local copies, waits for them, and re-layouts: 2.97 us -> 1.88 us
where the time goes in v4:
time: 60.6 us; the launch traced here: 60.4 us
  Pallas kernels  57.9 us (96%)
  local copies, waits for them, and re-layouts  1.88 us (3%)
  between operations  0.64 us (1%)
    pallas_call x1, Pallas kernels, fused(): pl.pallas_call(body, out_shape=(pltpu.VMEM((low_cols, channels), f32), pl...  57.9 us
    unnamed x3, local copies, waits for them, and re-layouts  1.88 us

profile of v4, /device:TPU:0, one launch (start us, length us, event | category | flops | bytes accessed | tf_op | source)
XLA Modules:
  0.0 60.4 jit_solution(6872960902415834153)
XLA Ops:
  0.6 57.9 %shard_map.76 = (f32[160,512]{1,0:T(8,128)S(1)}, f32[1,512]{1,0:T(1,128)S(1)}, f32[1,512]{1,0:T(1,128)S(1)}) custom-call(bf16[2,320,512]{2,1,0:T(8,128)(2,1)} %bitcast.11, bf16[27,64,128]{2,1,0:T(8,128)(2,1)} %bitcast.12, bf16[160,512]{1,0:T(8,128)(2,1)} %bitcast.13, f32[1,512]{1,0:T(1,128)} %bitcast.14, f32[1,512]{1,0:T(1,128)} %bitcast.15), custom_call_target="tpu_custom_call" | custom-call | flops 3397386240 | bytes 2097152 | tf_op jit(solution)/shard_map/pallas_call | solution.py:485
  58.5 0.7 %copy.11 = f32[1,1,160,512]{3,2,1,0:T(8,128)} copy(f32[1,1,160,512]{3,2,1,0:T(8,128)S(1)} %bitcast.8) | data formatting | bytes 655360
  59.3 0.6 copy.12
  59.8 0.6 copy.13

commit v5 on v4

--- a/solution.py
+++ b/solution.py
@@ -118,7 +118,7 @@
 def fused_kernel(
     frames, count, per_group, cells,
     ct, w, lat_hbm, gain_hbm, bias_hbm,
-    out, gain_out, bias_out,
+    out, sums_out,
     lat, gain, bias, acc, fine, wbuf, wcat, stack, pad, part, inbox, normed, slope, chan, member, st_rows, st_tm,
     local_sem, ct_send, ct_recv, rim_send, rim_recv, z_send, z_recv, sib_send, sib_recv,
     part_send, part_recv, sr_send, sr_recv, st_send, st_recv,
@@ -374,14 +374,11 @@
                         a, part_of * half : (part_of + 1) * half, tap * width : (tap + 1) * width
                     ] = wbuf[chip, part_of, 9 * a + tap]
             first_slot = (7, 4, 0)[a]
-            product = lax.dot_general(
-                stack[first_slot : first_slot + a + 2].reshape((a + 2) * 2 * low_cols, 9 * width),
-                wcat[a],
-                (((1,), (1,)), ((), ())),
-                preferred_element_type=jnp.float32,
-            )
             for t in range(a + 1, -1, -1):
-                total = product[2 * low_cols * t : 2 * low_cols * (t + 1)]
+                total = lax.dot_general(
+                    stack[first_slot + t], wcat[a], (((1,), (1,)), ((), ())),
+                    preferred_element_type=jnp.float32,
+                )
                 if a < 2:
                     total = total + acc[t]
                 if a > max(0, t - 1):
@@ -429,8 +426,7 @@
     rows_start(1, jnp.concatenate(sums, axis=1), jnp.concatenate(scaled_sums, axis=1))
     tm_start(1)
     totals = tm_finish(1)
-    bias_out[...] = totals[0:1] * (1.0 / cells)
-    gain_out[...] = totals[1:2] * (1.0 / cells)
+    sums_out[...] = totals * (1.0 / cells)
     means = group_totals(totals * gain[...], member[...]) * (1.0 / (cells * per_group))
     inv = chan[0:1]
     out[...] = inv * (out[...] * gain[...] - means[0:1] - normed[...] * means[1:2])
@@ -482,15 +478,14 @@
     )
     vmem = pl.BlockSpec(memory_space=pltpu.VMEM)
     products = chips * 9 * 2 * low_cols * 9 * width * 2 * half
-    grad, gain_grad, bias_grad = pl.pallas_call(
+    grad, sums = pl.pallas_call(
         body,
         out_shape=(
             pltpu.VMEM((low_cols, channels), f32),
-            pltpu.VMEM((1, channels), f32),
-            pltpu.VMEM((1, channels), f32),
+            pltpu.VMEM((8, channels), f32),
         ),
         in_specs=[pl.BlockSpec(memory_space=pltpu.HBM)] * 5,
-        out_specs=(vmem,) * 3,
+        out_specs=(vmem,) * 2,
         scratch_shapes=[
             pltpu.VMEM((low_cols, channels), bf16),
             pltpu.VMEM((1, channels), f32),
@@ -538,7 +533,7 @@
         norm_gain.reshape((1, channels)),
         norm_bias.reshape((1, channels)),
     )
-    return grad.reshape(latent.shape), gain_grad.reshape(-1), bias_grad.reshape(-1)
+    return grad.reshape(latent.shape), sums[1], sums[0]
 
 
 def on_device(latent, norm_gain, norm_bias, conv_weight, cotangent):

time: 60.6 us -> 58.9 us (0.972)
  Pallas kernels: 57.9 us -> 56.8 us
    unnamed x3 -> x1, local copies, waits for them, and re-layouts: 1.88 us -> 0.72 us
    pallas_call x1, Pallas kernels: 57.9 us -> 56.8 us  [fused(): pl.pallas_call(body, out_shape=(pltpu.VMEM((low_cols, channels), f32), pl...]
where the time goes in v5:
time: 58.9 us; the launch traced here: 58.8 us
  Pallas kernels  56.8 us (96%)
  local copies, waits for them, and re-layouts  1.31 us (2%)
  between operations  0.64 us (1%)
    pallas_call x1, Pallas kernels, fused(): pl.pallas_call(body, out_shape=(pltpu.VMEM((low_cols, channels), f32), pl...  56.8 us

profile of v5, /device:TPU:0, one launch (start us, length us, event | category | flops | bytes accessed | tf_op | source)
XLA Modules:
  0.0 58.8 jit_solution(17249159281216628250)
XLA Ops:
  0.6 56.8 %shard_map.76 = (f32[160,512]{1,0:T(8,128)S(1)}, f32[8,512]{1,0:T(8,128)S(1)}) custom-call(bf16[2,320,512]{2,1,0:T(8,128)(2,1)} %bitcast.11, bf16[27,64,128]{2,1,0:T(8,128)(2,1)} %bitcast.12, bf16[160,512]{1,0:T(8,128)(2,1)} %bitcast.13, f32[1,512]{1,0:T(1,128)} %bitcast.14, f32[1,512]{1,0:T(1,128)} %bitcast.15), custom_call_target="tpu_custom_call" | custom-call | flops 3397386240 | bytes 2097152 | tf_op jit(solution)/shard_map/pallas_call | solution.py:481
  57.5 0.6 fusion
  58.1 0.7 %copy.9 = f32[1,1,160,512]{3,2,1,0:T(8,128)} copy(f32[1,1,160,512]{3,2,1,0:T(8,128)S(1)} %bitcast.8) | data formatting | bytes 655360

commit v6 on v5

--- a/solution.py
+++ b/solution.py
@@ -119,9 +119,9 @@
     frames, count, per_group, cells,
     ct, w, lat_hbm, gain_hbm, bias_hbm,
     out, sums_out,
-    lat, gain, bias, acc, fine, wbuf, wcat, stack, pad, part, inbox, normed, slope, chan, member, st_rows, st_tm,
+    lat, gain, bias, acc, fine, wbuf, wcat, stack, pad, part, inbox, normed, slope, chan, member, st_all,
     local_sem, ct_send, ct_recv, rim_send, rim_recv, z_send, z_recv, sib_send, sib_recv,
-    part_send, part_recv, sr_send, sr_recv, st_send, st_recv,
+    part_send, part_recv, st_send, st_recv,
 ):
     chips = count // 2
     low_cols, channels = lat.shape
@@ -133,6 +133,8 @@
     z = lax.div(me_r, 2)
     core = lax.rem(me_r, 2)
     sibling = me_r + 1 - 2 * core
+    everyone = frames * count
+    me = me_t * count + me_r
 
     def remote(src, dst, send, recv, t, r):
         return pltpu.make_async_remote_copy(
@@ -185,42 +187,35 @@
             part_send.at[chip, d - 1], part_recv.at[chip, d - 1], t, me_r,
         )
 
-    def rows_copy(turn, d):
+    def peer(d):
+        index = lax.rem(me + d, everyone)
+        return lax.div(index, count), lax.rem(index, count)
+
+    def sums_copy(turn, d):
         return remote(
-            st_rows.at[turn, me_r], st_rows.at[turn, me_r],
-            sr_send.at[turn, d - 1], sr_recv.at[turn, d - 1], me_t, row_at(d),
-        )
-
-    def tm_copy(turn, d):
-        return remote(
-            st_tm.at[turn, me_t], st_tm.at[turn, me_t],
-            st_send.at[turn, d - 1], st_recv.at[turn, d - 1], frame_at(d), me_r,
-        )
-
-    def rows_start(turn, first, second):
-        st_rows[turn, me_r] = jnp.concatenate(
+            st_all.at[turn, me], st_all.at[turn, me],
+            st_send.at[turn, d - 1], st_recv.at[turn, d - 1], *peer(d),
+        )
+
+    def each_peer(action):
+        def step(d, carry):
+            action(d)
+            return carry
+
+        lax.fori_loop(1, everyone, step, 0)
+
+    def sums_start(turn, first, second):
+        st_all[turn, me] = jnp.concatenate(
             [line[:, k : k + 128] for line in (first, second) for k in range(0, channels, 128)],
             axis=0,
         )
-        for d in range(1, count):
-            rows_copy(turn, d).start()
-
-    def tm_start(turn):
-        for d in range(1, count):
-            rows_copy(turn, d).wait_recv()
-        total = st_rows[turn, 0]
-        for r in range(1, count):
-            total = total + st_rows[turn, r]
-        st_tm[turn, me_t] = total
-        for d in range(1, frames):
-            tm_copy(turn, d).start()
-
-    def tm_finish(turn):
-        for d in range(1, frames):
-            tm_copy(turn, d).wait_recv()
-        total = st_tm[turn, 0]
-        for t in range(1, frames):
-            total = total + st_tm[turn, t]
+        each_peer(lambda d: sums_copy(turn, d).start())
+
+    def sums_finish(turn):
+        each_peer(lambda d: sums_copy(turn, d).wait_recv())
+        total = st_all[turn, 0]
+        for k in range(1, everyone):
+            total = total + st_all[turn, k]
         lines = channels // 128
         first, second = (
             jnp.concatenate([total[k : k + 1] for k in range(start, start + lines)], axis=1)
@@ -243,11 +238,10 @@
     for copy in own:
         copy.start()
     barrier = pltpu.get_barrier_semaphore()
-    for d in range(1, count):
-        pl.semaphore_signal(barrier, inc=1, device_id=(me_t, row_at(d)), device_id_type=MESH)
-    for d in range(1, frames):
-        pl.semaphore_signal(barrier, inc=1, device_id=(frame_at(d), me_r), device_id_type=MESH)
-    pl.semaphore_wait(barrier, count + frames - 2)
+    each_peer(
+        lambda d: pl.semaphore_signal(barrier, inc=1, device_id=peer(d), device_id_type=MESH)
+    )
+    pl.semaphore_wait(barrier, everyone - 1)
 
     for side in range(2):
         to_chip = z + (1 if side == 0 else -1)
@@ -265,7 +259,7 @@
     for copy in own[:3]:
         copy.wait()
     features = lat[...].astype(jnp.float32)
-    rows_start(
+    sums_start(
         0,
         jnp.sum(features, axis=0, keepdims=True),
         jnp.sum(features * features, axis=0, keepdims=True),
@@ -299,7 +293,6 @@
     def _():
         rim_copy(1).start()
 
-    tm_start(0)
     own[4].wait()
 
     def arrive(step):
@@ -347,7 +340,7 @@
                         stack[slot, 0:low_cols, tap] = high
                         stack[slot, low_cols : 2 * low_cols, tap] = low
 
-        totals = tm_finish(0)
+        totals = sums_finish(0)
         scale = 1.0 / (cells * per_group)
         means = group_totals(totals, member[...]) * scale
         mean = means[0:1]
@@ -423,9 +416,8 @@
         out[:, span] = act
         sums.append(jnp.sum(act, axis=0, keepdims=True))
         scaled_sums.append(jnp.sum(act * normed[:, span], axis=0, keepdims=True))
-    rows_start(1, jnp.concatenate(sums, axis=1), jnp.concatenate(scaled_sums, axis=1))
-    tm_start(1)
-    totals = tm_finish(1)
+    sums_start(1, jnp.concatenate(sums, axis=1), jnp.concatenate(scaled_sums, axis=1))
+    totals = sums_finish(1)
     sums_out[...] = totals * (1.0 / cells)
     means = group_totals(totals * gain[...], member[...]) * (1.0 / (cells * per_group))
     inv = chan[0:1]
@@ -435,11 +427,8 @@
         ct_copy(d).wait_send()
         for chip in range(chips):
             part_copy(chip, d).wait_send()
-        for turn_index in range(2):
-            tm_copy(turn_index, d).wait_send()
-    for d in range(1, count):
-        for turn_index in range(2):
-            rows_copy(turn_index, d).wait_send()
+    for index in range(2):
+        each_peer(lambda d, index=index: sums_copy(index, d).wait_send())
 
     @pl.when(me_r > 0)
     def _():
@@ -502,8 +491,7 @@
             pltpu.VMEM((low_cols, channels), f32),
             pltpu.VMEM((8, channels), f32),
             pltpu.VMEM((channels, channels), bf16),
-            pltpu.VMEM((2, count, channels // 64, 128), f32),
-            pltpu.VMEM((2, frames, channels // 64, 128), f32),
+            pltpu.VMEM((2, frames * count, channels // 64, 128), f32),
             dma((5,)),
             dma((frames - 1,)),
             dma((frames - 1,)),
@@ -515,10 +503,8 @@
             dma((chips, 3)),
             dma((chips, frames - 1)),
             dma((chips, frames - 1)),
-            dma((2, count - 1)),
-            dma((2, count - 1)),
-            dma((2, frames - 1)),
-            dma((2, frames - 1)),
+            dma((2, frames * count - 1)),
+            dma((2, frames * count - 1)),
         ],
         compiler_params=pltpu.CompilerParams(
             collective_id=0, has_side_effects=True, vmem_limit_bytes=60 * 1024 * 1024

time: 58.9 us -> 61.6 us (1.046)
  Pallas kernels: 56.8 us -> 59.5 us
    pallas_call x1, Pallas kernels: 56.8 us -> 59.5 us  [fused(): pl.pallas_call(body, out_shape=(pltpu.VMEM((low_cols, channels), f32), pl...]
where the time goes in v6:
time: 61.6 us; the launch traced here: 61.5 us
  Pallas kernels  59.5 us (97%)
  local copies, waits for them, and re-layouts  1.31 us (2%)
  between operations  0.64 us (1%)
    pallas_call x1, Pallas kernels, fused(): pl.pallas_call(body, out_shape=(pltpu.VMEM((low_cols, channels), f32), pl...  59.5 us

profile of v6, /device:TPU:0, one launch (start us, length us, event | category | flops | bytes accessed | tf_op | source)
XLA Modules:
  0.0 61.5 jit_solution(213725418039814983)
XLA Ops:
  0.6 59.5 %shard_map.76 = (f32[160,512]{1,0:T(8,128)S(1)}, f32[8,512]{1,0:T(8,128)S(1)}) custom-call(bf16[2,320,512]{2,1,0:T(8,128)(2,1)} %bitcast.11, bf16[27,64,128]{2,1,0:T(8,128)(2,1)} %bitcast.12, bf16[160,512]{1,0:T(8,128)(2,1)} %bitcast.13, f32[1,512]{1,0:T(1,128)} %bitcast.14, f32[1,512]{1,0:T(1,128)} %bitcast.15), custom_call_target="tpu_custom_call" | custom-call | flops 3397386240 | bytes 2097152 | tf_op jit(solution)/shard_map/pallas_call | solution.py:470
  60.2 0.6 fusion
  60.7 0.7 %copy.9 = f32[1,1,160,512]{3,2,1,0:T(8,128)} copy(f32[1,1,160,512]{3,2,1,0:T(8,128)S(1)} %bitcast.8) | data formatting | bytes 655360
